TPU v7x, 256 devices: a whole 4x4x8 slice. The times are simulated.
256 devices in a mesh: dp: 8 (over x, z_lo), ctx: 32 (over y, z_hi, core).
Axes of the slice: x: 4, y: 4, z: 8 (z_hi: 4, z_lo: 2; z = z_hi * 2 + z_lo), core: 2. Of those that a mesh axis runs over, the one named last changes fastest.
Arguments:
- queries: bfloat16 [32768, 8192], P(('dp', 'ctx')), may hold values from -16 to 16
- out_grad: bfloat16 [32768, 8192], P(('dp', 'ctx')), may hold values from -6 to 6
- enc_states: bfloat16 [3072, 1024], P(('dp', 'ctx')), may hold values from -8 to 8
- w_key: bfloat16 [1024, 8192], P('dp', 'ctx'), may hold values from -1 to 1
- w_value: bfloat16 [1024, 8192], P('dp', 'ctx'), may hold values from -0.1875 to 0.1875
- dec_segments: int32 [32768], P(('dp', 'ctx')), may hold values from 0 to 3, as said below
- enc_segments: int32 [3072], P(('dp', 'ctx')), may hold values from 0 to 3, as said below
Outputs:
- query_grad: bfloat16 [32768, 8192], P(('dp', 'ctx'))
- enc_grad: bfloat16 [3072, 1024], P(('dp', 'ctx'))
- w_key_grad: float32 [1024, 8192], P('dp', 'ctx')
- w_value_grad: float32 [1024, 8192], P('dp', 'ctx')
Inputs may be any that keep to these rules, and one draw needn't show every extreme that they name: `dec_segments`: within each pack the ids never fall along the tokens, and each of the 4 ids has one or more decoder tokens in the pack. `enc_segments`: within each pack the ids never fall along the tokens, and each of the 4 ids has two or more encoder tokens in the pack.
All inputs are finite; a program needn't handle non-finite values.
Results may differ from a plain program's by a relative error of at most 0.019.
Values may be sent and summed in bfloat16 or wider, within the bound.
No kernel may reach another device: no remote copies, remote signals or barrier semaphores. Data moves between devices by JAX's collectives and lax.ppermute only.
A program may use at most 64 MiB of HBM per device.

v0:
```python
import math
import jax
import jax.numpy as jnp
from jax import lax
from jax.sharding import PartitionSpec as P

HEAD_DIM = 128


def side_by_side(arrays, axis, dim, along):
    ends, at = ([], 0)
    for a in arrays[:-1]:
        at += a.shape[along]
        ends.append(at)
    both = jnp.concatenate(arrays, axis=along)
    return tuple(jnp.split(lax.all_gather(both, axis, axis=dim, tiled=True), ends, axis=along))


def sent_to_all(value, axis):
    size = lax.axis_size(axis)
    return lax.all_to_all(
        jnp.broadcast_to(value[None], (size, *value.shape)), axis, 0, 0, tiled=True
    )


def joined_along(pieces, dim):
    pieces = jnp.moveaxis(pieces, 0, dim)
    lengths = pieces.shape
    return pieces.reshape(*lengths[:dim], lengths[dim] * lengths[dim + 1], *lengths[dim + 2 :])


def gathered_copies(value, axis, dim):
    pieces = sent_to_all(value, axis)
    return joined_along(pieces, dim)


def split_up(value, dim, size):
    lengths = value.shape
    pieces = value.reshape(*lengths[:dim], size, lengths[dim] // size, *lengths[dim + 1 :])
    return jnp.moveaxis(pieces, dim, 0)


def sum_at_owner(value, axis, dim):
    pieces = split_up(value, dim, lax.axis_size(axis))
    arrived = lax.all_to_all(pieces, axis, split_axis=0, concat_axis=0, tiled=True)
    return arrived.astype(jnp.float32).sum(axis=0)


def in_one_piece(arrays, axis, dim, along):
    ends, at = ([], 0)
    for a in arrays[:-1]:
        at += a.shape[along]
        ends.append(at)
    both = jnp.concatenate(arrays, axis=along)
    return tuple(
        jnp.split(lax.psum_scatter(both, axis, scatter_dimension=dim, tiled=True), ends, axis=along)
    )


def attend(queries, out_grads, key_rows, value_rows, query_ids, key_ids):
    length, full_width = queries.shape
    key_count = key_rows.shape[0]
    head_count = full_width // HEAD_DIM
    group_size = min(head_count, 16)
    column_count = group_size * HEAD_DIM
    row_count = math.gcd(length, 1024)

    def head_group(number):
        column_start = number * column_count
        key_block = key_rows.reshape(key_count, group_size, HEAD_DIM)
        value_block = value_rows.reshape(key_count, group_size, HEAD_DIM)

        def query_block(totals, block_number):
            first_row = block_number * row_count
            query_part = lax.dynamic_slice(
                queries, (first_row, column_start), (row_count, column_count)
            ).reshape(row_count, group_size, HEAD_DIM)
            grad_part = lax.dynamic_slice(
                out_grads, (first_row, column_start), (row_count, column_count)
            ).reshape(row_count, group_size, HEAD_DIM)
            block_ids = lax.dynamic_slice_in_dim(query_ids, first_row, row_count, 0)
            allowed = block_ids[:, None] == key_ids[None, :]
            scores = jnp.einsum(
                "qhd,khd->hqk", query_part, key_block, preferred_element_type=jnp.float32
            )
            scores = jnp.where(allowed[None], scores, -jnp.inf)
            highest = jnp.max(scores, axis=2, keepdims=True)
            weights = jnp.exp(scores - highest)
            probability = weights / jnp.sum(weights, axis=2, keepdims=True)
            upstream = jnp.einsum(
                "qhd,khd->hqk", grad_part, value_block, preferred_element_type=jnp.float32
            )
            row_dot = jnp.sum(probability * upstream, axis=2, keepdims=True)
            score_grad = (probability * (upstream - row_dot)).astype(jnp.bfloat16)
            rounded = probability.astype(jnp.bfloat16)
            key_total = totals[0] + jnp.einsum(
                "hqk,qhd->khd", score_grad, query_part, preferred_element_type=jnp.float32
            )
            value_total = totals[1] + jnp.einsum(
                "hqk,qhd->khd", rounded, grad_part, preferred_element_type=jnp.float32
            )
            totals = (key_total, value_total)
            query_grad = jnp.einsum(
                "hqk,khd->qhd", score_grad, key_block, preferred_element_type=jnp.float32
            ).astype(jnp.bfloat16)
            return (totals, query_grad.reshape(row_count, column_count))

        zeros = jnp.zeros((key_count, group_size, HEAD_DIM), jnp.float32)
        totals, query_grads = lax.scan(
            query_block, (zeros, zeros), jnp.arange(length // row_count, dtype=jnp.int32)
        )
        results = ()
        results = results + (query_grads.reshape(length, column_count),)
        results = results + (
            totals[0].reshape(key_count, column_count),
            totals[1].reshape(key_count, column_count),
        )
        return results

    pieces = lax.map(head_group, jnp.arange(head_count // group_size, dtype=jnp.int32))
    return tuple(
        (jnp.moveaxis(piece, 0, 1).reshape(piece.shape[1], full_width) for piece in pieces)
    )


def body(queries, out_grad, enc_states, w_key, w_value, dec_segments, enc_segments):
    encoder, key_ids = (
        lax.all_gather(enc_states, "ctx", axis=0, tiled=True),
        lax.all_gather(enc_segments, "ctx", axis=0, tiled=True),
    )
    key_weight, value_weight = side_by_side((w_key, w_value), "dp", 0, 1)
    key_part = jnp.dot(encoder, key_weight, preferred_element_type=jnp.float32).astype(jnp.bfloat16)
    value_part = jnp.dot(encoder, value_weight, preferred_element_type=jnp.float32).astype(
        jnp.bfloat16
    )
    local_queries, local_grads = (
        lax.all_to_all(queries, "ctx", split_axis=1, concat_axis=0, tiled=True),
        lax.all_to_all(out_grad, "ctx", split_axis=1, concat_axis=0, tiled=True),
    )
    query_ids = gathered_copies(dec_segments, "ctx", 0)
    head_grad, key_grad, value_grad = attend(
        local_queries, local_grads, key_part, value_part, query_ids, key_ids
    )
    query_grad = lax.all_to_all(head_grad, "ctx", split_axis=0, concat_axis=1, tiled=True)
    key_round = key_grad.astype(jnp.bfloat16)
    value_round = value_grad.astype(jnp.bfloat16)
    across = (((1,), (1,)), ((), ()))
    partial_value = lax.dot_general(
        key_round, key_weight, across, preferred_element_type=jnp.float32
    )
    partial_value = partial_value + lax.dot_general(
        value_round, value_weight, across, preferred_element_type=jnp.float32
    )
    enc_grad = sum_at_owner(partial_value.astype(jnp.bfloat16), "ctx", 0).astype(jnp.bfloat16)
    down = (((0,), (0,)), ((), ()))
    key_term = lax.dot_general(encoder, key_round, down, preferred_element_type=jnp.float32)
    value_term = lax.dot_general(encoder, value_round, down, preferred_element_type=jnp.float32)
    w_key_grad, w_value_grad = tuple(
        (
            part.astype(jnp.float32)
            for part in in_one_piece(
                (key_term.astype(jnp.bfloat16), value_term.astype(jnp.bfloat16)), "dp", 0, 1
            )
        )
    )
    return (query_grad, enc_grad, w_key_grad, w_value_grad)


def solution(mesh):
    in_specs = (
        P(("dp", "ctx"), None),
        P(("dp", "ctx"), None),
        P(("dp", "ctx"), None),
        P("dp", "ctx"),
        P("dp", "ctx"),
        P(("dp", "ctx")),
        P(("dp", "ctx")),
    )
    out_specs = (P(("dp", "ctx"), None), P(("dp", "ctx"), None), P("dp", "ctx"), P("dp", "ctx"))
    return jax.shard_map(body, mesh=mesh, in_specs=in_specs, out_specs=out_specs, check_vma=False)
```

profile of v0, /device:TPU:8, one launch (start us, length us, event | category | flops | bytes accessed | tf_op | source)
XLA Modules:
  0.0 417.5 jit_solution(9430888007886917703)
XLA Ops:
  7.2 4.1 copy.68
  11.2 11.7 %all-to-all-start = ((bf16[128,32,256]{0,2,1:T(8,128)(2,1)}), bf16[128,32,256]{0,2,1:T(8,128)(2,1)S(1)}, u32[]{:S(2)}, u32[]{:S(2)}) async-start(bf16[128,32,256]{0,2,1:T(8,128)(2,1)} %bitcast.99), calls=%async_computation | async-start | bytes 4194304 | tf_op jit(solution)/shard_map/all_to_all | solution.py:137
  22.9 4.1 copy.70
  27.1 44.4 %all-to-all-done = bf16[128,32,256]{0,2,1:T(8,128)(2,1)S(1)} async-done(((bf16[128,32,256]{0,2,1:T(8,128)(2,1)}), bf16[128,32,256]{0,2,1:T(8,128)(2,1)S(1)}, u32[]{:S(2)}, u32[]{:S(2)}) %all-to-all-start) | async-done | bytes 2097184 | tf_op jit(solution)/shard_map/all_to_all | solution.py:137
  72.8 7.6 %all-to-all-start.2 = ((bf16[128,32,256]{0,2,1:T(8,128)(2,1)}), bf16[128,32,256]{0,2,1:T(8,128)(2,1)}, u32[]{:S(2)}, u32[]{:S(2)}) async-start(bf16[128,32,256]{0,2,1:T(8,128)(2,1)} %bitcast.97), calls=%async_computation.2 | async-start | bytes 4194304 | tf_op jit(solution)/shard_map/all_to_all | solution.py:138
  81.2 96.0 %all-gather = bf16[32,12,1024]{2,1,0:T(8,128)(2,1)S(1)} all-gather(bf16[1,12,1024]{2,1,0:T(8,128)(2,1)S(1)} %bitcast.108), channel_id=1, replica_groups=mesh['dp'=8,'ctx'=32] {'ctx'}, dimensions={0}, use_global_device_ids=true | all-gather | bytes 811008 | tf_op jit(solution)/shard_map/all_gather | solution.py:128
  179.1 17.7 %all-reduce = s32[384]{0:T(512)S(1)} all-reduce(s32[384]{0:T(512)S(1)} %dynamic-update-slice), channel_id=1, replica_groups=mesh['dp'=8,'ctx'=32] {'ctx'}, use_global_device_ids=true, to_apply=%add | all-reduce | flops 384 | bytes 3072
  199.0 10.4 %all-to-all-start.1 = ((s32[32,1,128]{2,1,0:T(1,128)}), s32[32,1,128]{2,1,0:T(1,128)}, u32[]{:S(2)}, u32[]{:S(2)}) async-start(s32[32,1,128]{2,1,0:T(1,128)} %broadcast_in_dim.41), calls=%async_computation.1 | async-start | bytes 32768 | tf_op jit(solution)/shard_map/all_to_all | solution.py:21
  212.4 3.3 copy.69
  215.7 4.1 copy.71
  219.8 62.6 %while.27 = (s32[]{:T(128)}, f32[384,2,128]{0,2,1:T(8,128)S(1)}, f32[384,2,128]{0,2,1:T(8,128)}, bf16[4,1024,256]{2,1,0:T(8,128)(2,1)}, s32[4]{0:T(128)S(1)}, /*...) while((s32[]{:T(128)}, f32[384,2,128]{0,2,1:T(8,128)S(1)}, ...), condition=%wide.region_4.5_spmd.clone, body=%wide.region_0.4_spmd.clone.sunk | while | flops 1017117056 | bytes 58062732 | solution.py:109
  226.1 2.5 fusion.69
  228.7 2.6 fusion.71
  241.6 2.5 fusion.69
  244.2 2.7 fusion.71
  257.3 2.5 fusion.69
  259.9 2.7 fusion.71
  273.0 2.5 fusion.69
  275.6 2.7 fusion.71
  285.6 36.9 %all_to_all.68 = bf16[32,12,1024]{2,1,0:T(8,128)(2,1)} all-to-all(bf16[32,12,1024]{2,1,0:T(8,128)(2,1)S(1)} %reshape.98), channel_id=1, replica_groups=mesh['dp'=8,'ctx'=32] {'ctx'}, dimensions={0} | all-to-all | bytes 1572864 | tf_op jit(solution)/shard_map/all_to_all | solution.py:45
  322.5 6.9 %all-to-all-start.3 = ((bf16[32,128,256]{2,1,0:T(8,128)(2,1)}), bf16[32,128,256]{2,1,0:T(8,128)(2,1)S(1)}, u32[]{:S(2)}, u32[]{:S(2)}) async-start(bf16[32,128,256]{2,1,0:T(8,128)(2,1)} %bitcast.102), calls=%async_computation.3 | async-start | bytes 4194304 | tf_op jit(solution)/shard_map/all_to_all | solution.py:144
  334.7 66.3 %reduce-scatter.4.cloned.1.call-done = bf16[128,512]{1,0:T(8,128)(2,1)} async-done(((bf16[1024,512]{1,0:T(8,128)(2,1)}), bf16[128,512]{1,0:T(8,128)(2,1)}) %reduce-scatter.4.cloned.1.call-update) | async-done | bytes 131088
  403.7 2.9 copy.76
  406.6 4.1 copy.77
  (154 shorter events, 58.2 us)
Async XLA Ops:
  11.2 60.2 %all-to-all-start = ((bf16[128,32,256]{0,2,1:T(8,128)(2,1)}), bf16[128,32,256]{0,2,1:T(8,128)(2,1)S(1)}, u32[]{:S(2)}, u32[]{:S(2)}) async-start(bf16[128,32,256]{0,2,1:T(8,128)(2,1)} %bitcast.99), calls=%async_computation | async-start | bytes 4194304 | tf_op jit(solution)/shard_map/all_to_all | solution.py:137
  71.4 9.0 %copy-start.11 = (bf16[128,256]{1,0:T(8,128)(2,1)S(1)}, bf16[128,256]{1,0:T(8,128)(2,1)}, u32[]{:S(2)}) copy-start(bf16[128,256]{1,0:T(8,128)(2,1)} %param.13) | copy-start | bytes 196612
  71.4 9.1 %copy-start.12 = (bf16[128,256]{1,0:T(8,128)(2,1)S(1)}, bf16[128,256]{1,0:T(8,128)(2,1)}, u32[]{:S(2)}) copy-start(bf16[128,256]{1,0:T(8,128)(2,1)} %param.12) | copy-start | bytes 196612
  71.4 9.8 %copy-start.13 = (bf16[12,1024]{1,0:T(8,128)(2,1)S(1)}, bf16[12,1024]{1,0:T(8,128)(2,1)}, u32[]{:S(2)}) copy-start(bf16[12,1024]{1,0:T(8,128)(2,1)} %param.11) | copy-start | bytes 73732
  72.8 125.6 %all-to-all-start.2 = ((bf16[128,32,256]{0,2,1:T(8,128)(2,1)}), bf16[128,32,256]{0,2,1:T(8,128)(2,1)}, u32[]{:S(2)}, u32[]{:S(2)}) async-start(bf16[128,32,256]{0,2,1:T(8,128)(2,1)} %bitcast.97), calls=%async_computation.2 | async-start | bytes 4194304 | tf_op jit(solution)/shard_map/all_to_all | solution.py:138
  80.4 97.1 %copy-start.16 = (u32[256]{0:T(256)S(1)}, u32[256]{0:T(256)}, u32[]{:S(2)}) copy-start(u32[256]{0:T(256)} %constant.64) | copy-start | bytes 3076
  80.4 98.4 %copy-start.15 = (s32[12]{0:T(128)S(1)}, s32[12]{0:T(128)}, u32[]{:S(2)}) copy-start(s32[12]{0:T(128)} %param.15) | copy-start | bytes 148
  80.4 116.4 %all-gather.3.cloned.1.call-start = ((), (), s32[]{:S(2)}) async-start(), calls=%async_computation.6 | async-start | bytes 1179648 | tf_op jit(solution)/shard_map/all_gather | solution.py:16
  81.2 117.1 %copy-start.14 = (s32[128]{0:T(128)S(1)}, s32[128]{0:T(128)}, u32[]{:S(2)}) copy-start(s32[128]{0:T(128)} %param.14) | copy-start | bytes 1540
  177.5 38.2 %copy-start.5 = (bf16[384,1024]{1,0:T(8,128)(2,1)}, bf16[384,1024]{1,0:T(8,128)(2,1)S(1)}, u32[]{:S(2)}) copy-start(bf16[384,1024]{1,0:T(8,128)(2,1)S(1)} %reshape.103) | copy-start | bytes 2359300
  199.0 20.8 %all-to-all-start.1 = ((s32[32,1,128]{2,1,0:T(1,128)}), s32[32,1,128]{2,1,0:T(1,128)}, u32[]{:S(2)}, u32[]{:S(2)}) async-start(s32[32,1,128]{2,1,0:T(1,128)} %broadcast_in_dim.41), calls=%async_computation.1 | async-start | bytes 32768 | tf_op jit(solution)/shard_map/all_to_all | solution.py:21
  219.8 6.3 %copy-start.2 = (bf16[4096,256]{1,0:T(8,128)(2,1)}, bf16[4096,256]{1,0:T(8,128)(2,1)S(1)}, u32[]{:S(2)}) copy-start(bf16[4096,256]{1,0:T(8,128)(2,1)S(1)} %get-tuple-element.377) | copy-start | bytes 6291460 | tf_op jit(solution)/shard_map/while/body/eval_jaxpr/while
  235.4 6.3 %copy-start.2 = (bf16[4096,256]{1,0:T(8,128)(2,1)}, bf16[4096,256]{1,0:T(8,128)(2,1)S(1)}, u32[]{:S(2)}) copy-start(bf16[4096,256]{1,0:T(8,128)(2,1)S(1)} %get-tuple-element.377) | copy-start | bytes 6291460 | tf_op jit(solution)/shard_map/while/body/eval_jaxpr/while
  244.2 2.7 copy-start.1
  244.2 2.7 copy-start.10
  251.0 6.3 %copy-start.2 = (bf16[4096,256]{1,0:T(8,128)(2,1)}, bf16[4096,256]{1,0:T(8,128)(2,1)S(1)}, u32[]{:S(2)}) copy-start(bf16[4096,256]{1,0:T(8,128)(2,1)S(1)} %get-tuple-element.377) | copy-start | bytes 6291460 | tf_op jit(solution)/shard_map/while/body/eval_jaxpr/while
  259.9 2.7 copy-start.1
  259.9 2.7 copy-start.10
  266.7 6.3 %copy-start.2 = (bf16[4096,256]{1,0:T(8,128)(2,1)}, bf16[4096,256]{1,0:T(8,128)(2,1)S(1)}, u32[]{:S(2)}) copy-start(bf16[4096,256]{1,0:T(8,128)(2,1)S(1)} %get-tuple-element.377) | copy-start | bytes 6291460 | tf_op jit(solution)/shard_map/while/body/eval_jaxpr/while
  275.5 2.7 copy-start.1
  275.6 2.7 copy-start.10
  322.5 7.0 %copy-start.6 = (bf16[384,1024]{1,0:T(8,128)(2,1)S(1)}, bf16[384,1024]{1,0:T(8,128)(2,1)}, u32[]{:S(2)}) copy-start(bf16[384,1024]{1,0:T(8,128)(2,1)} %copy-done.5) | copy-start | bytes 2359300
  322.5 81.2 %all-to-all-start.3 = ((bf16[32,128,256]{2,1,0:T(8,128)(2,1)}), bf16[32,128,256]{2,1,0:T(8,128)(2,1)S(1)}, u32[]{:S(2)}, u32[]{:S(2)}) async-start(bf16[32,128,256]{2,1,0:T(8,128)(2,1)} %bitcast.102), calls=%async_computation.3 | async-start | bytes 4194304 | tf_op jit(solution)/shard_map/all_to_all | solution.py:144
  329.5 71.6 %reduce-scatter.4.cloned.1.call-start = ((), (), s32[]{:S(2)}) async-start(), calls=%async_computation.7 | async-start | bytes 1179648
  (17 other events, 25.7 us)
Sparse Core Ops, SparseCore 0:
  83.6 70.4 all-gather.2
  334.0 66.9 reduce-scatter.3
where the time goes:
time: 419 us; the launch traced here: 417 us
  blocking collectives  151 us (36%)
  waiting for transfers between devices  111 us (26%)
  local copies, waits for them, and re-layouts  56.4 us (13%)
  starting transfers between devices  36.7 us (9%)
  matrix products  33.8 us (8%)
  between operations  15 us (4%)
  other arithmetic  11.1 us (3%)
    all_gather x1, blocking collectives, body(): lax.all_gather(enc_states, 'ctx', axis=0, tiled=True)  96 us
    unnamed x3, waiting for transfers between devices  66.4 us
    all_to_all x1, waiting for transfers between devices, body(): lax.all_to_all(queries, 'ctx', split_axis=1, concat_axis=0, tiled=True)  44.4 us
    all_to_all x1, blocking collectives, sum_at_owner(): lax.all_to_all(pieces, axis, split_axis=0, concat_axis=0, tiled=True)  36.9 us
    unnamed x35, local copies, waits for them, and re-layouts  19.7 us
    unnamed x1, blocking collectives  17.7 us
    all_to_all x1, starting transfers between devices, body(): lax.all_to_all(queries, 'ctx', split_axis=1, concat_axis=0, tiled=True)  11.7 us
    dot_general x4, matrix products, query_block(): jnp.einsum('hqk,qhd->khd', rounded, grad_part, preferred_element_type=jnp...  10.5 us
  transfers between devices with their start and end apart: 6, of which 2 were waited for; matrix products, arithmetic and copies ran while one was open for 6% of the time, Pallas kernels for 0%

commit v1 on v0

--- a/solution.py
+++ b/solution.py
@@ -135,7 +135,12 @@
     )
     local_queries, local_grads = (
         lax.all_to_all(queries, "ctx", split_axis=1, concat_axis=0, tiled=True),
-        lax.all_to_all(out_grad, "ctx", split_axis=1, concat_axis=0, tiled=True),
+        jnp.concatenate(
+            lax.all_to_all(
+                jnp.stack(jnp.split(out_grad, lax.axis_size("ctx"), axis=1)), "ctx", 0, 0
+            ),
+            axis=0,
+        ),
     )
     query_ids = gathered_copies(dec_segments, "ctx", 0)
     head_grad, key_grad, value_grad = attend(

time: 419 us -> 446 us (1.064)
  local copies, waits for them, and re-layouts: 56.4 us -> 98.2 us
  waiting for transfers between devices: 111 us -> 87.8 us
    unnamed x35 -> x57, local copies, waits for them, and re-layouts: 19.7 us -> 62.3 us
    all_to_all x1, waiting for transfers between devices: 44.4 us -> 22 us  [body(): lax.all_to_all(queries, 'ctx', split_axis=1, concat_axis=0, tiled=True)]
  transfers between devices with their start and end apart: 6 -> 6, of which waited for: 2 -> 2; matrix products, arithmetic and copies ran while one was open for 6% -> 16% of each run, Pallas kernels for 0% -> 0%
where the time goes in v1:
time: 446 us; the launch traced here: 442 us
  blocking collectives  154 us (35%)
  local copies, waits for them, and re-layouts  98.2 us (22%)
  waiting for transfers between devices  87.8 us (20%)
  starting transfers between devices  36 us (8%)
  matrix products  33.8 us (8%)
  between operations  14.9 us (3%)
  other arithmetic  14.7 us (3%)
    all_gather x1, blocking collectives, body(): lax.all_gather(enc_states, 'ctx', axis=0, tiled=True)  98.6 us
    unnamed x3, waiting for transfers between devices  65.9 us
    unnamed x57, local copies, waits for them, and re-layouts  62.3 us
    all_to_all x1, blocking collectives, sum_at_owner(): lax.all_to_all(pieces, axis, split_axis=0, concat_axis=0, tiled=True)  37.2 us
    all_to_all x1, waiting for transfers between devices, body(): lax.all_to_all(queries, 'ctx', split_axis=1, concat_axis=0, tiled=True)  22 us
    unnamed x1, blocking collectives  17.9 us
    all_to_all x1, starting transfers between devices, sent_to_all(): lax.all_to_all(jnp.broadcast_to(value[None], (size, *value.shape)), axis,...  11.7 us
    dot_general x4, matrix products, query_block(): jnp.einsum('hqk,qhd->khd', rounded, grad_part, preferred_element_type=jnp...  10.4 us
  transfers between devices with their start and end apart: 6, of which 2 were waited for; matrix products, arithmetic and copies ran while one was open for 16% of the time, Pallas kernels for 0%

profile of v1, /device:TPU:8, one launch (start us, length us, event | category | flops | bytes accessed | tf_op | source)
XLA Modules:
  0.0 442.2 jit_solution(5791476317525853190)
XLA Ops:
  8.4 11.7 %all-to-all-start.1 = ((s32[32,1,128]{2,1,0:T(1,128)}), s32[32,1,128]{2,1,0:T(1,128)S(1)}, u32[]{:S(2)}, u32[]{:S(2)}) async-start(s32[32,1,128]{2,1,0:T(1,128)} %broadcast_in_dim.41), calls=%async_computation.1 | async-start | bytes 32768 | tf_op jit(solution)/shard_map/all_to_all | solution.py:21
  40.7 4.1 copy.67
  44.8 9.8 %all-to-all-start = ((bf16[128,32,256]{0,2,1:T(8,128)(2,1)}), bf16[128,32,256]{0,2,1:T(8,128)(2,1)S(1)}, u32[]{:S(2)}, u32[]{:S(2)}) async-start(bf16[128,32,256]{0,2,1:T(8,128)(2,1)} %bitcast.159), calls=%async_computation | async-start | bytes 4194304 | tf_op jit(solution)/shard_map/all_to_all | solution.py:137
  81.1 22.0 %all-to-all-done = bf16[128,32,256]{0,2,1:T(8,128)(2,1)S(1)} async-done(((bf16[128,32,256]{0,2,1:T(8,128)(2,1)}), bf16[128,32,256]{0,2,1:T(8,128)(2,1)S(1)}, u32[]{:S(2)}, u32[]{:S(2)}) %all-to-all-start) | async-done | bytes 2097184 | tf_op jit(solution)/shard_map/all_to_all | solution.py:137
  104.4 7.6 %all-to-all-start.2 = ((bf16[32,128,256]{2,1,0:T(8,128)(2,1)}), bf16[32,128,256]{2,1,0:T(8,128)(2,1)S(1)}, u32[]{:S(2)}, u32[]{:S(2)}) async-start(bf16[32,128,256]{2,1,0:T(8,128)(2,1)} %constant_dynamic-update-slice_fusion.1), calls=%async_computation.2 | async-start | bytes 4194304 | tf_op jit(solution)/shard_map/all_to_all | solution.py:139
  113.7 98.6 %all-gather = bf16[32,12,1024]{2,1,0:T(8,128)(2,1)} all-gather(bf16[1,12,1024]{2,1,0:T(8,128)(2,1)} %bitcast.169), channel_id=1, replica_groups=mesh['dp'=8,'ctx'=32] {'ctx'}, dimensions={0}, use_global_device_ids=true | all-gather | bytes 811008 | tf_op jit(solution)/shard_map/all_gather | solution.py:128
  215.2 17.9 %all-reduce = s32[384]{0:T(512)} all-reduce(s32[384]{0:T(512)S(1)} %dynamic-update-slice), channel_id=1, replica_groups=mesh['dp'=8,'ctx'=32] {'ctx'}, use_global_device_ids=true, to_apply=%add | all-reduce | flops 384 | bytes 3072
  235.5 2.2 convolution_convert_fusion.4
  237.7 4.1 copy.68
  242.3 65.1 %while.27 = (s32[]{:T(128)}, f32[384,2,128]{0,2,1:T(8,128)S(1)}, f32[384,2,128]{0,2,1:T(8,128)}, bf16[4,1024,256]{2,1,0:T(8,128)(2,1)}, s32[4]{0:T(128)}, /*inde...) while((s32[]{:T(128)}, f32[384,2,128]{0,2,1:T(8,128)S(1)}, ...), condition=%wide.region_4.5_spmd.clone, body=%wide.region_0.4_spmd.clone.sunk | while | flops 1017117056 | bytes 58193860 | solution.py:109
  249.2 2.5 fusion.69
  251.8 2.5 fusion.71
  265.4 2.5 fusion.69
  268.0 2.6 fusion.71
  281.8 2.5 fusion.69
  284.3 2.6 fusion.71
  298.1 2.5 fusion.69
  300.6 2.6 fusion.71
  310.6 37.2 %all_to_all.54 = bf16[32,12,1024]{2,1,0:T(8,128)(2,1)} all-to-all(bf16[32,12,1024]{2,1,0:T(8,128)(2,1)S(1)} %reshape.99), channel_id=1, replica_groups=mesh['dp'=8,'ctx'=32] {'ctx'}, dimensions={0} | all-to-all | bytes 1572864 | tf_op jit(solution)/shard_map/all_to_all | solution.py:45
  347.8 6.9 %all-to-all-start.3 = ((bf16[32,128,256]{2,1,0:T(8,128)(2,1)}), bf16[32,128,256]{2,1,0:T(8,128)(2,1)S(1)}, u32[]{:S(2)}, u32[]{:S(2)}) async-start(bf16[32,128,256]{2,1,0:T(8,128)(2,1)} %bitcast.162), calls=%async_computation.3 | async-start | bytes 4194304 | tf_op jit(solution)/shard_map/all_to_all | solution.py:149
  356.7 2.4 copy.84
  360.0 65.8 %reduce-scatter.4.cloned.1.call-done = bf16[128,512]{1,0:T(8,128)(2,1)} async-done(((bf16[1024,512]{1,0:T(8,128)(2,1)}), bf16[128,512]{1,0:T(8,128)(2,1)}) %reduce-scatter.4.cloned.1.call-update) | async-done | bytes 131088
  428.5 2.9 copy.73
  431.3 4.1 copy.74
  (192 shorter events, 106.4 us)
Async XLA Ops:
  8.4 36.4 %all-to-all-start.1 = ((s32[32,1,128]{2,1,0:T(1,128)}), s32[32,1,128]{2,1,0:T(1,128)S(1)}, u32[]{:S(2)}, u32[]{:S(2)}) async-start(s32[32,1,128]{2,1,0:T(1,128)} %broadcast_in_dim.41), calls=%async_computation.1 | async-start | bytes 32768 | tf_op jit(solution)/shard_map/all_to_all | solution.py:21
  44.8 58.3 %all-to-all-start = ((bf16[128,32,256]{0,2,1:T(8,128)(2,1)}), bf16[128,32,256]{0,2,1:T(8,128)(2,1)S(1)}, u32[]{:S(2)}, u32[]{:S(2)}) async-start(bf16[128,32,256]{0,2,1:T(8,128)(2,1)} %bitcast.159), calls=%async_computation | async-start | bytes 4194304 | tf_op jit(solution)/shard_map/all_to_all | solution.py:137
  104.4 137.4 %all-to-all-start.2 = ((bf16[32,128,256]{2,1,0:T(8,128)(2,1)}), bf16[32,128,256]{2,1,0:T(8,128)(2,1)S(1)}, u32[]{:S(2)}, u32[]{:S(2)}) async-start(bf16[32,128,256]{2,1,0:T(8,128)(2,1)} %constant_dynamic-update-slice_fusion.1), calls=%async_computation.2 | async-start | bytes 4194304 | tf_op jit(solution)/shard_map/all_to_all | solution.py:139
  112.0 101.6 %copy-start.14 = (u32[256]{0:T(256)S(1)}, u32[256]{0:T(256)}, u32[]{:S(2)}) copy-start(u32[256]{0:T(256)} %constant.64) | copy-start | bytes 3076
  112.0 102.9 %copy-start.13 = (s32[12]{0:T(128)S(1)}, s32[12]{0:T(128)}, u32[]{:S(2)}) copy-start(s32[12]{0:T(128)} %param.15) | copy-start | bytes 148
  112.0 121.1 %all-gather.3.cloned.1.call-start = ((), (), s32[]{:S(2)}) async-start(), calls=%async_computation.6 | async-start | bytes 1179648 | tf_op jit(solution)/shard_map/all_gather | solution.py:16
  213.6 28.2 %copy-start.5 = (bf16[384,1024]{1,0:T(8,128)(2,1)}, bf16[384,1024]{1,0:T(8,128)(2,1)S(1)}, u32[]{:S(2)}) copy-start(bf16[384,1024]{1,0:T(8,128)(2,1)S(1)} %reshape.104) | copy-start | bytes 2359300
  242.3 6.9 %copy-start.2 = (bf16[4096,256]{1,0:T(8,128)(2,1)}, bf16[4096,256]{1,0:T(8,128)(2,1)S(1)}, u32[]{:S(2)}) copy-start(bf16[4096,256]{1,0:T(8,128)(2,1)S(1)} %get-tuple-element.381) | copy-start | bytes 6291460 | tf_op jit(solution)/shard_map/while/body/eval_jaxpr/while
  242.3 6.9 %copy-start.11 = (s32[4096]{0:T(1024)}, s32[4096]{0:T(1024)S(1)}, u32[]{:S(2)}) copy-start(s32[4096]{0:T(1024)S(1)} %get-tuple-element.378) | copy-start | bytes 49156 | tf_op jit(solution)/shard_map/while/body/eval_jaxpr/while
  258.5 6.9 %copy-start.2 = (bf16[4096,256]{1,0:T(8,128)(2,1)}, bf16[4096,256]{1,0:T(8,128)(2,1)S(1)}, u32[]{:S(2)}) copy-start(bf16[4096,256]{1,0:T(8,128)(2,1)S(1)} %get-tuple-element.381) | copy-start | bytes 6291460 | tf_op jit(solution)/shard_map/while/body/eval_jaxpr/while
  258.5 6.9 %copy-start.11 = (s32[4096]{0:T(1024)}, s32[4096]{0:T(1024)S(1)}, u32[]{:S(2)}) copy-start(s32[4096]{0:T(1024)S(1)} %get-tuple-element.378) | copy-start | bytes 49156 | tf_op jit(solution)/shard_map/while/body/eval_jaxpr/while
  268.0 2.7 copy-start.1
  268.0 2.7 copy-start.10
  274.8 6.9 %copy-start.2 = (bf16[4096,256]{1,0:T(8,128)(2,1)}, bf16[4096,256]{1,0:T(8,128)(2,1)S(1)}, u32[]{:S(2)}) copy-start(bf16[4096,256]{1,0:T(8,128)(2,1)S(1)} %get-tuple-element.381) | copy-start | bytes 6291460 | tf_op jit(solution)/shard_map/while/body/eval_jaxpr/while
  274.8 6.9 %copy-start.11 = (s32[4096]{0:T(1024)}, s32[4096]{0:T(1024)S(1)}, u32[]{:S(2)}) copy-start(s32[4096]{0:T(1024)S(1)} %get-tuple-element.378) | copy-start | bytes 49156 | tf_op jit(solution)/shard_map/while/body/eval_jaxpr/while
  284.3 2.7 copy-start.1
  284.3 2.7 copy-start.10
  291.1 6.9 %copy-start.2 = (bf16[4096,256]{1,0:T(8,128)(2,1)}, bf16[4096,256]{1,0:T(8,128)(2,1)S(1)}, u32[]{:S(2)}) copy-start(bf16[4096,256]{1,0:T(8,128)(2,1)S(1)} %get-tuple-element.381) | copy-start | bytes 6291460 | tf_op jit(solution)/shard_map/while/body/eval_jaxpr/while
  291.1 6.9 %copy-start.11 = (s32[4096]{0:T(1024)}, s32[4096]{0:T(1024)S(1)}, u32[]{:S(2)}) copy-start(s32[4096]{0:T(1024)S(1)} %get-tuple-element.378) | copy-start | bytes 49156 | tf_op jit(solution)/shard_map/while/body/eval_jaxpr/while
  300.6 2.7 copy-start.1
  300.6 2.6 copy-start.10
  347.8 7.0 %copy-start.6 = (bf16[384,1024]{1,0:T(8,128)(2,1)S(1)}, bf16[384,1024]{1,0:T(8,128)(2,1)}, u32[]{:S(2)}) copy-start(bf16[384,1024]{1,0:T(8,128)(2,1)} %copy-done.5) | copy-start | bytes 2359300
  347.8 80.6 %all-to-all-start.3 = ((bf16[32,128,256]{2,1,0:T(8,128)(2,1)}), bf16[32,128,256]{2,1,0:T(8,128)(2,1)S(1)}, u32[]{:S(2)}, u32[]{:S(2)}) async-start(bf16[32,128,256]{2,1,0:T(8,128)(2,1)} %bitcast.162), calls=%async_computation.3 | async-start | bytes 4194304 | tf_op jit(solution)/shard_map/all_to_all | solution.py:149
  354.7 71.1 %reduce-scatter.4.cloned.1.call-start = ((), (), s32[]{:S(2)}) async-start(), calls=%async_computation.7 | async-start | bytes 1179648
  (21 other events, 32.1 us)
Sparse Core Ops, SparseCore 0:
  115.2 69.6 all-gather.2
  359.3 66.4 reduce-scatter.3
